TPU v7x, 32 devices: a whole 2x2x4 slice. The times are simulated.
32 devices in a mesh: sub: 16 (over z, y, x), rhs: 2 (over core).
Axes of the slice: x: 2, y: 2, z: 4, core: 2. Of those that a mesh axis runs over, the one named last changes fastest.
Arguments:
- schur_block: bfloat16 [32, 1024, 1024], P('sub', 'rhs'), may hold values from -1 to 4, as said below
- scaling: float32 [32, 1024], P('sub'), may hold values from 0.25 to 1.75
- gravity_load: float32 [32, 1024, 256], P('sub', None, 'rhs'), may hold values from -100 to 100
- pressure: bfloat16 [1024, 4, 256], P('sub', None, 'rhs'), may hold values from -6 to 6
- block_target: int32 [1024, 1], P('sub'), may hold values from 0 to 31; in each aligned block of 64 rows (0 to 63, 64 to 127, ...) at most 4 rows name the same one
- aero_interp: float32 [4, 1024], replicated, may hold values from -0.5 to 0.5
- partner_slot: int32 [4, 32], P(None, 'sub'), may hold values from 0 to 1, as said below
- corner_row: int32 [32, 8], P('sub'), may hold values from 0 to 1023
- corner_coarse: int32 [32, 8], P('sub'), may hold values from 0 to 127
- coarse_inverse: float32 [128, 128], P('sub'), may hold values from -1 to 6, as said below
Outputs:
- solution: float32 [32, 1024, 256], P('sub', None, 'rhs')
Inputs may be any that keep to these rules, and one draw needn't show every extreme that they name: `block_target`: at most 4 of the blocks of one device name the same subdomain; in some device's blocks one subdomain is named exactly 4 times; every subdomain is named by some block. In round k, subdomain s on device d = s // 2 is paired with subdomain (d xor 2^k) * 2 + partner_slot[k, s]; the pairing is mutual. `schur_block`: each matrix is symmetric. `coarse_inverse`: symmetric.
All inputs are finite; a program needn't handle non-finite values.
Results may differ from a plain program's by a relative error of at most 0.0027.
Values may be sent and summed in bfloat16 or wider, within the bound.
A program may use at most 64 MiB of HBM per device.

v0:
```python
import jax
import jax.numpy as jnp
from jax import lax
from jax.sharding import PartitionSpec as P

SUB_DEV = 2
FACES = 4
MOST = 4
ITERS = 2
FW = 256
coupling = 2.0


def swapped(shard, axis, distance):
    return lax.ppermute(shard, axis, [(i, i ^ 1 << distance) for i in range(lax.axis_size(axis))])


def schur_apply(schur_block, rounded):
    half_rows = jnp.einsum(
        "snm,smc->snc",
        schur_block,
        lax.all_gather(rounded, "rhs", axis=2, tiled=True),
        preferred_element_type=jnp.float32,
    )
    return lax.all_to_all(half_rows, "rhs", split_axis=2, concat_axis=1, tiled=True)


def jump_terms(rounded, partner_slot):
    face_terms = []
    for face_index in range(FACES):
        own_face = rounded[:, face_index * FW : (face_index + 1) * FW, :]
        partner_face = swapped(own_face, "sub", face_index)
        select = (
            partner_slot[face_index][:, None] == jnp.arange(SUB_DEV, dtype=jnp.int32)[None, :]
        ).astype(jnp.bfloat16)
        picked = jnp.einsum("sj,jfc->sfc", select, partner_face, preferred_element_type=jnp.float32)
        face_terms.append(coupling * (own_face.astype(jnp.float32) - picked))
    return jnp.concatenate(face_terms, axis=1)


def operator(direction, schur_block, partner_slot):
    rounded = direction.astype(jnp.bfloat16)
    return schur_apply(schur_block, rounded) + jump_terms(rounded, partner_slot)


def coarse_solve(coarse, coarse_inverse):
    own_rows = jnp.dot(coarse_inverse, coarse, precision=lax.Precision.HIGHEST)
    return lax.all_gather(own_rows, "sub", axis=0, tiled=True)


def add_corners(solved, corner_row, corner_coarse, residual):
    sub_rows = jnp.arange(SUB_DEV, dtype=jnp.int32)[:, None]
    return jnp.zeros_like(residual).at[sub_rows, corner_row].add(solved[corner_coarse])


def precondition(residual, schur_block, scaling, corner_row, corner_coarse, coarse_inverse):
    columns = residual.shape[2]
    weight_col = scaling[:, :, None]
    dirichlet = weight_col * schur_apply(schur_block, (weight_col * residual).astype(jnp.bfloat16))
    sub_rows = jnp.arange(SUB_DEV, dtype=jnp.int32)[:, None]
    picked = residual[sub_rows, corner_row]
    partial_sum = (
        jnp.zeros((coarse_inverse.shape[1], columns), jnp.float32)
        .at[corner_coarse.reshape(-1)]
        .add(picked.reshape(-1, columns))
    )
    coarse = lax.psum(partial_sum, "sub")
    solved = coarse_solve(coarse, coarse_inverse)
    precond = dirichlet + add_corners(solved, corner_row, corner_coarse, residual)
    product_value = lax.psum(jnp.sum(residual * precond, axis=(0, 1)), "sub")
    return (precond, product_value)


def on_device(
    schur_block,
    scaling,
    gravity_load,
    pressure,
    block_target,
    aero_interp,
    partner_slot,
    corner_row,
    corner_coarse,
    coarse_inverse,
):
    sub_count = lax.axis_size("sub")
    all_subdomains = SUB_DEV * sub_count
    columns = gravity_load.shape[2]
    points = pressure.shape[1]
    target = block_target[:, 0]
    matches = target[:, None] == target[None, :]
    before = jnp.tril(matches, -1)
    rank_in = jnp.sum(before, axis=1, dtype=jnp.int32)
    slot_index = target * MOST + rank_in
    buffer = (
        jnp.zeros((all_subdomains * MOST, points, columns), jnp.bfloat16)
        .at[slot_index]
        .set(pressure)
    )
    arrived = lax.all_to_all(buffer, "sub", split_axis=0, concat_axis=0, tiled=True)
    load_sum = jnp.sum(
        arrived.reshape(sub_count, SUB_DEV, MOST, points, columns), axis=(0, 2), dtype=jnp.float32
    )
    force_total = gravity_load + jnp.einsum(
        "pm,spc->smc", aero_interp, load_sum, precision=lax.Precision.HIGHEST
    )
    solution = jnp.zeros_like(force_total)
    residual = force_total
    precond, precond_dot = precondition(
        residual, schur_block, scaling, corner_row, corner_coarse, coarse_inverse
    )
    direction = precond
    for step_index in range(ITERS):
        applied = operator(direction, schur_block, partner_slot)
        curvature = lax.psum(jnp.sum(direction * applied, axis=(0, 1)), "sub")
        step_size = precond_dot / curvature
        solution = solution + step_size * direction
        residual = residual - step_size * applied
        if step_index + 1 < ITERS:
            precond, next_product = precondition(
                residual, schur_block, scaling, corner_row, corner_coarse, coarse_inverse
            )
            direction = precond + next_product / precond_dot * direction
            precond_dot = next_product
    return solution


def solution(mesh):
    return jax.shard_map(
        on_device,
        mesh=mesh,
        in_specs=(
            P("sub", "rhs", None),
            P("sub", None),
            P("sub", None, "rhs"),
            P("sub", None, "rhs"),
            P("sub", None),
            P(),
            P(None, "sub"),
            P("sub", None),
            P("sub", None),
            P("sub", None),
        ),
        out_specs=P("sub", None, "rhs"),
        check_vma=False,
    )
```

profile of v0, /device:TPU:0, one launch (start us, length us, event | category | flops | bytes accessed | tf_op | source)
XLA Modules:
  0.0 575.2 jit_solution(14376807275874382460)
XLA Ops:
  9.7 7.6 %scatter_fusion = bf16[128,4,128]{2,1,0:T(4,128)(2,1)} fusion(bf16[128,4,128]{2,1,0:T(4,128)(2,1)} %broadcast_in_dim.12, s32[64]{0:T(128)S(1)} %fusion.22, bf16[64,4,128]{2,1,0:T(4,128)(2,1)} %param.13), kind=kCustom, calls=%fused_computation.4 | custom fusion | bytes 196864 | tf_op jit(solution)/shard_map/scatter | solution.py:98
  17.3 8.3 %all-to-all-start = ((bf16[128,4,128]{2,1,0:T(4,128)(2,1)}), bf16[128,4,128]{2,1,0:T(4,128)(2,1)S(1)}, u32[]{:S(2)}, u32[]{:S(2)}) async-start(bf16[128,4,128]{2,1,0:T(4,128)(2,1)} %scatter_fusion), calls=%async_computation | async-start | bytes 262144 | tf_op jit(solution)/shard_map/all_to_all | solution.py:100
  27.2 2.5 copy.107
  29.7 3.7 all-to-all-done
  33.5 3.1 multiply_convert_fusion.1
  37.9 2.1 scatter_custom_fusion.1
  40.8 98.9 %all-reduce.4.cloned.1.call-done = f32[128,128]{1,0:T(8,128)} async-done(((f32[128,128]{1,0:T(8,128)}), f32[128,128]{1,0:T(8,128)}) %all-reduce.4.cloned.1.call-update) | async-done | bytes 65552 | tf_op jit(solution)/shard_map/psum | solution.py:67
  140.7 39.1 %all_gather.19 = f32[128,128]{1,0:T(8,128)S(1)} all-gather(f32[8,128]{1,0:T(8,128)S(1)} %convolution_bitcast_fusion.6), channel_id=1, replica_groups=mesh['sub'=16,'rhs'=2] {'sub'}, dimensions={0}, use_global_device_ids=true | all-gather | bytes 69632 | tf_op jit(solution)/shard_map/all_gather | solution.py:48
  180.4 2.0 convolution_bitcast_fusion.3
  183.2 4.6 all_to_all.77
  187.8 1.8 copy.151
  189.6 2.1 all_to_all.59
  192.8 2.6 copy.111
  195.4 2.2 scatter_fusion.1
  200.1 1.9 fusion.34
  204.5 3.0 collective-permute-done
  220.9 2.3 subtract_multiply_fusion.7
  223.2 2.0 convolution_bitcast_fusion.2
  226.0 4.6 all_to_all.78
  230.6 1.8 copy.150
  232.4 3.2 all_to_all.63
  235.5 2.0 multiply_reduce_fusion.1
  237.6 39.5 %all-reduce = (f32[128]{0:T(128)S(1)}, f32[128]{0:T(128)S(1)}) all-reduce(f32[128]{0:T(128)S(1)} %get-tuple-element.6, f32[128]{0:T(128)S(1)} %get-tuple-element.5), channel_id=1, replica_groups=mesh['sub'=16,'rhs'=2] {'sub'}, use_global_device_ids=true, to_apply=%region_7.8 | all-reduce | flops 256 | bytes 2048 | tf_op jit(solution)/shard_map/psum | solution.py:70
  277.1 3.3 multiply_convert_fusion
  280.3 2.5 copy.128
  282.9 2.1 scatter_custom_fusion.3
  285.6 97.4 %all-reduce.6.cloned.1.call-done = f32[128,128]{1,0:T(8,128)} async-done(((f32[128,128]{1,0:T(8,128)}), f32[128,128]{1,0:T(8,128)}) %all-reduce.6.cloned.1.call-update) | async-done | bytes 65552 | tf_op jit(solution)/shard_map/psum | solution.py:67
  384.0 39.1 %all_gather.22 = f32[128,128]{1,0:T(8,128)S(1)} all-gather(f32[8,128]{1,0:T(8,128)S(1)} %convolution_bitcast_fusion.5), channel_id=1, replica_groups=mesh['sub'=16,'rhs'=2] {'sub'}, dimensions={0}, use_global_device_ids=true | all-gather | bytes 69632 | tf_op jit(solution)/shard_map/all_gather | solution.py:48
  423.9 2.0 convolution_bitcast_fusion.1
  426.6 4.6 all_to_all.79
  431.2 1.8 copy.149
  433.0 3.1 all_to_all.67
  436.1 2.4 broadcast_multiply_fusion
  438.5 2.6 copy.129
  441.1 2.2 scatter_fusion.2
  443.3 2.5 copy.130
  447.6 36.9 %psum.46 = f32[128]{0:T(128)S(1)} all-reduce(f32[128]{0:T(128)S(1)} %multiply_reduce_fusion), channel_id=1, replica_groups=mesh['sub'=16,'rhs'=2] {'sub'}, use_global_device_ids=true, to_apply=%region_14.15 | all-reduce | flops 128 | bytes 1024 | tf_op jit(solution)/shard_map/psum | solution.py:70
  484.5 2.2 fusion.32
  486.6 1.9 fusion.33
  488.5 2.0 collective-permute-start.4
  507.3 2.3 subtract_multiply_fusion.3
  509.7 2.0 convolution_bitcast_fusion
  512.5 4.6 all_to_all.80
  518.8 3.2 all_to_all.71
  522.0 2.1 fusion.2
  524.1 38.5 %psum.47 = f32[128]{0:T(128)S(1)} all-reduce(f32[128]{0:T(128)S(1)} %fusion.2), channel_id=1, replica_groups=mesh['sub'=16,'rhs'=2] {'sub'}, use_global_device_ids=true, to_apply=%region_16.17 | all-reduce | flops 128 | bytes 1024 | tf_op jit(solution)/shard_map/psum | solution.py:115
  562.6 2.5 multiply_add_fusion
  565.1 2.5 copy.143
  (119 shorter events, 53.0 us)
Async XLA Ops:
  7.4 173.0 %copy-start = (bf16[2,512,1024]{2,1,0:T(8,128)(2,1)S(1)}, bf16[2,512,1024]{2,1,0:T(8,128)(2,1)}, u32[]{:S(2)}) copy-start(bf16[2,512,1024]{2,1,0:T(8,128)(2,1)} %param.10) | copy-start | bytes 6291460
  7.4 26.1 %copy-start.2 = (f32[2,1024]{1,0:T(2,128)S(1)}, f32[2,1024]{1,0:T(2,128)}, u32[]{:S(2)}) copy-start(f32[2,1024]{1,0:T(2,128)} %param.11) | copy-start | bytes 24580
  7.4 26.1 %copy-start.5 = (f32[4,1024]{1,0:T(4,128)S(1)}, f32[4,1024]{1,0:T(4,128)}, u32[]{:S(2)}) copy-start(f32[4,1024]{1,0:T(4,128)} %param.15) | copy-start | bytes 49156
  17.3 16.1 %all-to-all-start = ((bf16[128,4,128]{2,1,0:T(4,128)(2,1)}), bf16[128,4,128]{2,1,0:T(4,128)(2,1)S(1)}, u32[]{:S(2)}, u32[]{:S(2)}) async-start(bf16[128,4,128]{2,1,0:T(4,128)(2,1)} %scatter_fusion), calls=%async_computation | async-start | bytes 262144 | tf_op jit(solution)/shard_map/all_to_all | solution.py:100
  25.6 114.1 %all-reduce.4.cloned.1.call-start = ((), (), s32[]{:S(2)}) async-start(), calls=%async_computation.6 | async-start | bytes 131072 | tf_op jit(solution)/shard_map/psum | solution.py:67
  27.2 10.7 %copy-start.13 = (s32[16]{0:T(128)}, s32[16]{0:T(128)S(1)}, u32[]{:S(2)}) copy-start(s32[16]{0:T(128)S(1)} %reshape.57) | copy-start | bytes 196
  29.7 8.2 %copy-start.14 = (s32[16]{0:T(128)}, s32[16]{0:T(128)S(1)}, u32[]{:S(2)}) copy-start(s32[16]{0:T(128)S(1)} %fusion.23) | copy-start | bytes 196
  33.5 7.1 %copy-start.9 = (s32[2,8]{1,0:T(2,128)S(1)}, s32[2,8]{1,0:T(2,128)}, u32[]{:S(2)}) copy-start(s32[2,8]{1,0:T(2,128)} %param.18) | copy-start | bytes 196
  33.5 106.2 %copy-start.3 = (f32[8,128]{1,0:T(8,128)S(1)}, f32[8,128]{1,0:T(8,128)}, u32[]{:S(2)}) copy-start(f32[8,128]{1,0:T(8,128)} %param.19) | copy-start | bytes 12292
  36.6 145.8 %copy-start.1 = (f32[2,1024,128]{1,2,0:T(8,128)}, f32[2,1024,128]{1,2,0:T(8,128)S(1)}, u32[]{:S(2)}) copy-start(f32[2,1024,128]{1,2,0:T(8,128)S(1)} %get-tuple-element.34) | copy-start | bytes 3145732
  40.0 140.4 %all-gather.5.cloned.1.call-start = ((), (), s32[]{:S(2)}) async-start(), calls=%async_computation.5 | async-start | bytes 1572864 | tf_op jit(solution)/shard_map/all_gather | solution.py:22
  40.6 182.6 %all-gather.7.cloned.1.call-start = ((), (), s32[]{:S(2)}) async-start(), calls=%async_computation.7 | async-start | bytes 1572864 | tf_op jit(solution)/shard_map/all_gather | solution.py:22
  40.8 141.6 %copy-start.6 = (s32[1024]{0:T(1024)}, s32[1024]{0:T(1024)S(1)}, u32[]{:S(2)}) copy-start(s32[1024]{0:T(1024)S(1)} %pad_clamp_fusion) | copy-start | bytes 12292
  197.6 4.3 copy-start.4
  201.9 5.5 collective-permute-start
  202.8 180.3 %all-reduce.6.cloned.1.call-start = ((), (), s32[]{:S(2)}) async-start(), calls=%async_computation.9 | async-start | bytes 131072 | tf_op jit(solution)/shard_map/psum | solution.py:67
  203.0 7.3 %collective-permute-start.3 = (bf16[2,256,128]{1,2,0:T(8,128)(2,1)}, bf16[2,256,128]{1,2,0:T(8,128)(2,1)}, u32[]{:S(2)}, u32[]{:S(2)}) collective-permute-start(bf16[2,256,128]{1,2,0:T(8,128)(2,1)} %get-tuple-element.28), channel_id=1, source_target_pairs={{0,16},{2,18},{4,20},{6,22},{8,24},{10,26},{12,28},{14,30},{16,0},... | collective-permute-start | bytes 393224 | tf_op jit(solution)/shard_map/ppermute | solution.py:15
  203.1 11.1 %collective-permute-start.2 = (bf16[2,256,128]{1,2,0:T(8,128)(2,1)}, bf16[2,256,128]{1,2,0:T(8,128)(2,1)}, u32[]{:S(2)}, u32[]{:S(2)}) collective-permute-start(bf16[2,256,128]{1,2,0:T(8,128)(2,1)} %get-tuple-element.29), channel_id=1, source_target_pairs={{0,8},{2,10},{4,12},{6,14},{8,0},{10,2},{12,4},{14,6},{16,24},{18,... | collective-permute-start | bytes 393224 | tf_op jit(solution)/shard_map/ppermute | solution.py:15
  203.2 14.8 %collective-permute-start.1 = (bf16[2,256,128]{1,2,0:T(8,128)(2,1)}, bf16[2,256,128]{1,2,0:T(8,128)(2,1)S(1)}, u32[]{:S(2)}, u32[]{:S(2)}) collective-permute-start(bf16[2,256,128]{1,2,0:T(8,128)(2,1)} %get-tuple-element.30), channel_id=1, source_target_pairs={{0,4},{2,6},{4,0},{6,2},{8,12},{10,14},{12,8},{14,10},{16,20},{18,... | collective-permute-start | bytes 393224 | tf_op jit(solution)/shard_map/ppermute | solution.py:15
  277.1 3.3 copy-start.7
  285.0 138.8 %all-gather.9.cloned.1.call-start = ((), (), s32[]{:S(2)}) async-start(), calls=%async_computation.8 | async-start | bytes 1572864 | tf_op jit(solution)/shard_map/all_gather | solution.py:22
  285.6 224.1 %all-gather.11.cloned.1.call-start = ((), (), s32[]{:S(2)}) async-start(), calls=%async_computation.10 | async-start | bytes 1572864 | tf_op jit(solution)/shard_map/all_gather | solution.py:22
  484.4 4.0 copy-start.15
  486.6 11.9 %copy-start.12 = (s32[2]{0:T(128)S(1)}, s32[2]{0:T(128)}, u32[]{:S(2)}) copy-start(s32[2]{0:T(128)} %get-tuple-element.9) | copy-start | bytes 28
  486.6 15.7 %copy-start.11 = (s32[2]{0:T(128)S(1)}, s32[2]{0:T(128)}, u32[]{:S(2)}) copy-start(s32[2]{0:T(128)} %get-tuple-element.10) | copy-start | bytes 28
  488.5 5.0 collective-permute-start.4
  490.5 6.4 %collective-permute-start.7 = (bf16[2,256,128]{1,2,0:T(8,128)(2,1)}, bf16[2,256,128]{1,2,0:T(8,128)(2,1)}, u32[]{:S(2)}, u32[]{:S(2)}) collective-permute-start(bf16[2,256,128]{1,2,0:T(8,128)(2,1)} %get-tuple-element.20), channel_id=1, source_target_pairs={{0,16},{2,18},{4,20},{6,22},{8,24},{10,26},{12,28},{14,30},{16,0},... | collective-permute-start | bytes 393224 | tf_op jit(solution)/shard_map/ppermute | solution.py:15
  490.6 10.1 %collective-permute-start.6 = (bf16[2,256,128]{1,2,0:T(8,128)(2,1)}, bf16[2,256,128]{1,2,0:T(8,128)(2,1)}, u32[]{:S(2)}, u32[]{:S(2)}) collective-permute-start(bf16[2,256,128]{1,2,0:T(8,128)(2,1)} %get-tuple-element.21), channel_id=1, source_target_pairs={{0,8},{2,10},{4,12},{6,14},{8,0},{10,2},{12,4},{14,6},{16,24},{18,... | collective-permute-start | bytes 393224 | tf_op jit(solution)/shard_map/ppermute | solution.py:15
  490.7 14.5 %copy-start.10 = (s32[2]{0:T(128)S(1)}, s32[2]{0:T(128)}, u32[]{:S(2)}) copy-start(s32[2]{0:T(128)} %get-tuple-element.8) | copy-start | bytes 28
  490.7 13.7 %collective-permute-start.5 = (bf16[2,256,128]{1,2,0:T(8,128)(2,1)}, bf16[2,256,128]{1,2,0:T(8,128)(2,1)S(1)}, u32[]{:S(2)}, u32[]{:S(2)}) collective-permute-start(bf16[2,256,128]{1,2,0:T(8,128)(2,1)} %get-tuple-element.22), channel_id=1, source_target_pairs={{0,4},{2,6},{4,0},{6,2},{8,12},{10,14},{12,8},{14,10},{16,20},{18,... | collective-permute-start | bytes 393224 | tf_op jit(solution)/shard_map/ppermute | solution.py:15
  522.0 40.6 %copy-start.16 = (f32[128]{0:T(128)S(1)}, f32[128]{0:T(128)}, u32[]{:S(2)}) copy-start(f32[128]{0:T(128)} %copy-done.15) | copy-start | bytes 1540
  522.0 40.6 %copy-start.8 = (f32[128]{0:T(128)S(1)}, f32[128]{0:T(128)}, u32[]{:S(2)}) copy-start(f32[128]{0:T(128)} %copy-done.7) | copy-start | bytes 1540
Sparse Core Ops, SparseCore 0:
  40.1 99.5 all-reduce.3
  285.1 97.8 all-reduce.5
Sparse Core Ops, SparseCore 1:
  42.0 6.5 all-gather.4
  202.9 6.7 all-gather.6
  287.1 4.7 all-gather.8
  490.6 5.2 all-gather.10
where the time goes:
time: 577 us; the launch traced here: 575 us
  blocking collectives  211 us (37%)
  waiting for transfers between devices  206 us (36%)
  local copies, waits for them, and re-layouts  71.9 us (12%)
  other arithmetic  33.9 us (6%)
  matrix products  23 us (4%)
  between operations  15.4 us (3%)
  starting transfers between devices  13.9 us (2%)
    psum x2, waiting for transfers between devices, precondition(): coarse = lax.psum(partial_sum, 'sub')  196 us
    all_gather x2, blocking collectives, coarse_solve(): return lax.all_gather(own_rows, 'sub', axis=0, tiled=True)  78.2 us
    psum x2, blocking collectives, precondition(): product_value = lax.psum(jnp.sum(residual * precond, axis=(0, 1)), 'sub')  76.4 us
    psum x1, blocking collectives, on_device(): curvature = lax.psum(jnp.sum(direction * applied, axis=(0, 1)), 'sub')  38.5 us
    all_to_all x8, local copies, waits for them, and re-layouts, schur_apply(): lax.all_to_all(half_rows, 'rhs', split_axis=2, concat_axis=1, tiled=True)  18.7 us
    all_to_all x4, blocking collectives, schur_apply(): lax.all_to_all(half_rows, 'rhs', split_axis=2, concat_axis=1, tiled=True)  18.3 us
  transfers between devices with their start and end apart: 15, of which 6 were waited for; matrix products, arithmetic and copies ran while one was open for 7% of the time, Pallas kernels for 0%

commit v1 on v0

--- a/solution.py
+++ b/solution.py
@@ -9,6 +9,22 @@
 ITERS = 2
 FW = 256
 coupling = 2.0
+
+
+def collect(x, axis, dim):
+    ways, here, turn = (lax.axis_size(axis), lax.axis_index(axis), x.shape[dim])
+    lengths = [n * ways if d == dim else n for d, n in enumerate(x.shape)]
+    full = lax.dynamic_update_slice_in_dim(jnp.zeros(lengths, x.dtype), x, here * turn, axis=dim)
+    going_up = going_down = x
+    for far in range(1, ways // 2 + 1):
+        going_up = lax.ppermute(going_up, axis, [(d, (d + 1) % ways) for d in range(ways)])
+        full = lax.dynamic_update_slice_in_dim(full, going_up, (here - far) % ways * turn, axis=dim)
+        if 2 * far < ways:
+            going_down = lax.ppermute(going_down, axis, [(d, (d - 1) % ways) for d in range(ways)])
+            full = lax.dynamic_update_slice_in_dim(
+                full, going_down, (here + far) % ways * turn, axis=dim
+            )
+    return full
 
 
 def swapped(shard, axis, distance):
@@ -45,7 +61,7 @@
 
 def coarse_solve(coarse, coarse_inverse):
     own_rows = jnp.dot(coarse_inverse, coarse, precision=lax.Precision.HIGHEST)
-    return lax.all_gather(own_rows, "sub", axis=0, tiled=True)
+    return collect(own_rows, "sub", 0)
 
 
 def add_corners(solved, corner_row, corner_coarse, residual):

time: 577 us -> 612 us (1.061)
  starting transfers between devices: 13.9 us -> 93.5 us
  blocking collectives: 211 us -> 133 us
  waiting for transfers between devices: 206 us -> 241 us
    ppermute x0 -> x30, starting transfers between devices: none -> 79.5 us  [the longest x14 76.6 us: collect(): lax.ppermute(going_down, axis, [(d, (d - 1) % ways) for d in range(ways)])]
    all_gather x2 -> x0, blocking collectives: 78.2 us -> none  [coarse_solve(): return lax.all_gather(own_rows, 'sub', axis=0, tiled=True)]
    ppermute x0 -> x30, waiting for transfers between devices: none -> 35.4 us  [the longest x16 35.4 us: collect(): lax.ppermute(going_up, axis, [(d, (d + 1) % ways) for d in range(ways)])]
  transfers between devices with their start and end apart: 15 -> 45, of which waited for: 6 -> 21; matrix products, arithmetic and copies ran while one was open for 7% -> 6% of each run, Pallas kernels for 0% -> 0%
where the time goes in v1:
time: 612 us; the launch traced here: 610 us
  waiting for transfers between devices  241 us (39%)
  blocking collectives  133 us (22%)
  starting transfers between devices  93.5 us (15%)
  local copies, waits for them, and re-layouts  68.4 us (11%)
  other arithmetic  34.9 us (6%)
  matrix products  23 us (4%)
  between operations  15.5 us (3%)
    psum x2, waiting for transfers between devices, precondition(): coarse = lax.psum(partial_sum, 'sub')  198 us
    ppermute x14, starting transfers between devices, collect(): lax.ppermute(going_down, axis, [(d, (d - 1) % ways) for d in range(ways)])  76.6 us
    psum x2, blocking collectives, precondition(): product_value = lax.psum(jnp.sum(residual * precond, axis=(0, 1)), 'sub')  76 us
    psum x1, blocking collectives, on_device(): curvature = lax.psum(jnp.sum(direction * applied, axis=(0, 1)), 'sub')  39 us
    ppermute x16, waiting for transfers between devices, collect(): lax.ppermute(going_up, axis, [(d, (d + 1) % ways) for d in range(ways)])  35.4 us
    all_to_all x4, blocking collectives, schur_apply(): lax.all_to_all(half_rows, 'rhs', split_axis=2, concat_axis=1, tiled=True)  18.3 us
    all_to_all x8, local copies, waits for them, and re-layouts, schur_apply(): lax.all_to_all(half_rows, 'rhs', split_axis=2, concat_axis=1, tiled=True)  17.3 us
  transfers between devices with their start and end apart: 45, of which 21 were waited for; matrix products, arithmetic and copies ran while one was open for 6% of the time, Pallas kernels for 0%

profile of v1, /device:TPU:0, one launch (start us, length us, event | category | flops | bytes accessed | tf_op | source)
XLA Modules:
  0.0 609.7 jit_solution(1924146612380288647)
XLA Ops:
  9.7 6.8 %scatter_fusion = bf16[128,4,128]{2,1,0:T(4,128)(2,1)} fusion(bf16[128,4,128]{2,1,0:T(4,128)(2,1)} %broadcast_in_dim.12, s32[64]{0:T(128)S(1)} %fusion.22, bf16[64,4,128]{2,1,0:T(4,128)(2,1)} %param.13), kind=kCustom, calls=%fused_computation.4 | custom fusion | bytes 196864 | tf_op jit(solution)/shard_map/scatter | solution.py:114
  16.6 8.3 %all-to-all-start = ((bf16[128,4,128]{2,1,0:T(4,128)(2,1)}), bf16[128,4,128]{2,1,0:T(4,128)(2,1)S(1)}, u32[]{:S(2)}, u32[]{:S(2)}) async-start(bf16[128,4,128]{2,1,0:T(4,128)(2,1)} %scatter_fusion), calls=%async_computation | async-start | bytes 262144 | tf_op jit(solution)/shard_map/all_to_all | solution.py:116
  27.1 2.5 copy.107
  29.8 2.9 all-to-all-done
  32.8 3.1 multiply_convert_fusion.1
  39.4 100.4 %all-reduce.4.cloned.1.call-done = f32[128,128]{1,0:T(8,128)} async-done(((f32[128,128]{1,0:T(8,128)}), f32[128,128]{1,0:T(8,128)}) %all-reduce.4.cloned.1.call-update) | async-done | bytes 65552 | tf_op jit(solution)/shard_map/psum | solution.py:83
  142.3 4.2 collective-permute-start.1
  148.0 5.6 collective-permute-start.3
  155.2 5.6 collective-permute-start.5
  162.4 5.6 collective-permute-start.7
  169.6 5.6 collective-permute-start.9
  176.8 5.6 collective-permute-start.11
  184.0 5.6 collective-permute-start.13
  191.2 7.2 %collective-permute-done.14 = f32[8,128]{1,0:T(8,128)S(1)} collective-permute-done((f32[8,128]{1,0:T(8,128)S(1)}, f32[8,128]{1,0:T(8,128)S(1)}, u32[]{:S(2)}, u32[]{:S(2)}) %collective-permute-start.14) | collective-permute-done | bytes 4128 | tf_op jit(solution)/shard_map/ppermute | solution.py:20
  201.9 4.6 all_to_all.77
  211.8 2.3 scatter_fusion.1
  220.9 3.0 collective-permute-done.15
  237.2 2.4 subtract_multiply_fusion.7
  242.4 4.6 all_to_all.78
  248.8 3.1 all_to_all.63
  253.9 39.5 %all-reduce = (f32[128]{0:T(128)S(1)}, f32[128]{0:T(128)S(1)}) all-reduce(f32[128]{0:T(128)S(1)} %get-tuple-element.6, f32[128]{0:T(128)S(1)} %get-tuple-element.5), channel_id=1, replica_groups=mesh['sub'=16,'rhs'=2] {'sub'}, use_global_device_ids=true, to_apply=%region_7.8 | all-reduce | flops 256 | bytes 2048 | tf_op jit(solution)/shard_map/psum | solution.py:86
  293.4 3.3 multiply_convert_fusion
  296.7 2.6 copy.128
  299.2 2.1 scatter_custom_fusion.3
  301.4 97.9 %all-reduce.6.cloned.1.call-done = f32[128,128]{1,0:T(8,128)} async-done(((f32[128,128]{1,0:T(8,128)}), f32[128,128]{1,0:T(8,128)}) %all-reduce.6.cloned.1.call-update) | async-done | bytes 65552 | tf_op jit(solution)/shard_map/psum | solution.py:83
  401.9 4.2 collective-permute-start.20
  407.5 5.7 collective-permute-start.22
  414.7 5.7 collective-permute-start.24
  421.9 5.7 collective-permute-start.26
  429.1 5.7 collective-permute-start.28
  436.4 5.7 collective-permute-start.30
  443.6 5.7 collective-permute-start.32
  450.8 7.2 %collective-permute-done.33 = f32[8,128]{1,0:T(8,128)S(1)} collective-permute-done((f32[8,128]{1,0:T(8,128)S(1)}, f32[8,128]{1,0:T(8,128)S(1)}, u32[]{:S(2)}, u32[]{:S(2)}) %collective-permute-start.33) | collective-permute-done | bytes 4128 | tf_op jit(solution)/shard_map/ppermute | solution.py:20
  461.5 4.6 all_to_all.79
  467.9 3.1 all_to_all.67
  471.0 2.4 broadcast_multiply_fusion
  473.4 2.5 copy.129
  475.9 2.2 scatter_fusion.2
  478.1 2.6 copy.130
  482.4 36.6 %psum.46 = f32[128]{0:T(128)S(1)} all-reduce(f32[128]{0:T(128)S(1)} %multiply_reduce_fusion), channel_id=1, replica_groups=mesh['sub'=16,'rhs'=2] {'sub'}, use_global_device_ids=true, to_apply=%region_14.15 | all-reduce | flops 128 | bytes 1024 | tf_op jit(solution)/shard_map/psum | solution.py:86
  518.9 2.2 fusion.32
  523.0 2.2 collective-permute-start.34
  541.4 2.3 subtract_multiply_fusion.3
  546.5 4.6 all_to_all.80
  552.9 3.1 all_to_all.71
  558.1 39.0 %psum.47 = f32[128]{0:T(128)S(1)} all-reduce(f32[128]{0:T(128)S(1)} %fusion.2), channel_id=1, replica_groups=mesh['sub'=16,'rhs'=2] {'sub'}, use_global_device_ids=true, to_apply=%region_16.17 | all-reduce | flops 128 | bytes 1024 | tf_op jit(solution)/shard_map/psum | solution.py:131
  597.1 2.5 multiply_add_fusion
  599.6 2.5 copy.143
  (207 shorter events, 101.8 us)
Async XLA Ops:
  7.4 191.7 %copy-start = (bf16[2,512,1024]{2,1,0:T(8,128)(2,1)S(1)}, bf16[2,512,1024]{2,1,0:T(8,128)(2,1)}, u32[]{:S(2)}) copy-start(bf16[2,512,1024]{2,1,0:T(8,128)(2,1)} %param.10) | copy-start | bytes 6291460
  16.6 16.1 %all-to-all-start = ((bf16[128,4,128]{2,1,0:T(4,128)(2,1)}), bf16[128,4,128]{2,1,0:T(4,128)(2,1)S(1)}, u32[]{:S(2)}, u32[]{:S(2)}) async-start(bf16[128,4,128]{2,1,0:T(4,128)(2,1)} %scatter_fusion), calls=%async_computation | async-start | bytes 262144 | tf_op jit(solution)/shard_map/all_to_all | solution.py:116
  24.9 114.9 %all-reduce.4.cloned.1.call-start = ((), (), s32[]{:S(2)}) async-start(), calls=%async_computation.6 | async-start | bytes 131072 | tf_op jit(solution)/shard_map/psum | solution.py:83
  35.9 165.1 %copy-start.1 = (f32[2,1024,128]{1,2,0:T(8,128)}, f32[2,1024,128]{1,2,0:T(8,128)S(1)}, u32[]{:S(2)}) copy-start(f32[2,1024,128]{1,2,0:T(8,128)S(1)} %get-tuple-element.34) | copy-start | bytes 3145732
  39.3 159.7 %all-gather.5.cloned.1.call-start = ((), (), s32[]{:S(2)}) async-start(), calls=%async_computation.5 | async-start | bytes 1572864 | tf_op jit(solution)/shard_map/all_gather | solution.py:38
  39.4 161.7 %copy-start.6 = (s32[1024]{0:T(1024)}, s32[1024]{0:T(1024)S(1)}, u32[]{:S(2)}) copy-start(s32[1024]{0:T(1024)S(1)} %pad_clamp_fusion) | copy-start | bytes 12292
  140.8 7.2 %collective-permute-start = (f32[8,128]{1,0:T(8,128)S(1)}, f32[8,128]{1,0:T(8,128)S(1)}, u32[]{:S(2)}, u32[]{:S(2)}) collective-permute-start(f32[8,128]{1,0:T(8,128)S(1)} %get-tuple-element.36), channel_id=1, source_target_pairs={{0,2},{2,4},{4,6},{6,8},{8,10},{10,12},{12,14},{14,16},{16,18},{18... | collective-permute-start | bytes 12296 | tf_op jit(solution)/shard_map/ppermute | solution.py:20
  142.3 5.8 collective-permute-start.1
  146.5 93.1 %all-gather.7.cloned.1.call-start = ((), (), s32[]{:S(2)}) async-start(), calls=%async_computation.7 | async-start | bytes 1572864 | tf_op jit(solution)/shard_map/all_gather | solution.py:38
  148.0 7.2 %collective-permute-start.2 = (f32[8,128]{1,0:T(8,128)S(1)}, f32[8,128]{1,0:T(8,128)S(1)}, u32[]{:S(2)}, u32[]{:S(2)}) collective-permute-start(f32[8,128]{1,0:T(8,128)S(1)} %collective-permute-done), channel_id=1, source_target_pairs={{0,2},{2,4},{4,6},{6,8},{8,10},{10,12},{12,14},{14,16},{16,18},{18... | collective-permute-start | bytes 12296 | tf_op jit(solution)/shard_map/ppermute | solution.py:20
  148.0 7.2 %collective-permute-start.3 = (f32[8,128]{1,0:T(8,128)S(1)}, f32[8,128]{1,0:T(8,128)S(1)}, u32[]{:S(2)}, u32[]{:S(2)}) collective-permute-start(f32[8,128]{1,0:T(8,128)S(1)} %collective-permute-done.1), channel_id=1, source_target_pairs={{0,30},{2,0},{4,2},{6,4},{8,6},{10,8},{12,10},{14,12},{16,14},{18,... | collective-permute-start | bytes 12296 | tf_op jit(solution)/shard_map/ppermute | solution.py:23
  155.2 7.2 %collective-permute-start.4 = (f32[8,128]{1,0:T(8,128)S(1)}, f32[8,128]{1,0:T(8,128)S(1)}, u32[]{:S(2)}, u32[]{:S(2)}) collective-permute-start(f32[8,128]{1,0:T(8,128)S(1)} %collective-permute-done.2), channel_id=1, source_target_pairs={{0,2},{2,4},{4,6},{6,8},{8,10},{10,12},{12,14},{14,16},{16,18},{18... | collective-permute-start | bytes 12296 | tf_op jit(solution)/shard_map/ppermute | solution.py:20
  155.2 7.2 %collective-permute-start.5 = (f32[8,128]{1,0:T(8,128)S(1)}, f32[8,128]{1,0:T(8,128)S(1)}, u32[]{:S(2)}, u32[]{:S(2)}) collective-permute-start(f32[8,128]{1,0:T(8,128)S(1)} %collective-permute-done.3), channel_id=1, source_target_pairs={{0,30},{2,0},{4,2},{6,4},{8,6},{10,8},{12,10},{14,12},{16,14},{18,... | collective-permute-start | bytes 12296 | tf_op jit(solution)/shard_map/ppermute | solution.py:23
  162.4 7.2 %collective-permute-start.6 = (f32[8,128]{1,0:T(8,128)S(1)}, f32[8,128]{1,0:T(8,128)S(1)}, u32[]{:S(2)}, u32[]{:S(2)}) collective-permute-start(f32[8,128]{1,0:T(8,128)S(1)} %collective-permute-done.4), channel_id=1, source_target_pairs={{0,2},{2,4},{4,6},{6,8},{8,10},{10,12},{12,14},{14,16},{16,18},{18... | collective-permute-start | bytes 12296 | tf_op jit(solution)/shard_map/ppermute | solution.py:20
  162.4 7.2 %collective-permute-start.7 = (f32[8,128]{1,0:T(8,128)S(1)}, f32[8,128]{1,0:T(8,128)S(1)}, u32[]{:S(2)}, u32[]{:S(2)}) collective-permute-start(f32[8,128]{1,0:T(8,128)S(1)} %collective-permute-done.5), channel_id=1, source_target_pairs={{0,30},{2,0},{4,2},{6,4},{8,6},{10,8},{12,10},{14,12},{16,14},{18,... | collective-permute-start | bytes 12296 | tf_op jit(solution)/shard_map/ppermute | solution.py:23
  169.6 7.2 %collective-permute-start.8 = (f32[8,128]{1,0:T(8,128)S(1)}, f32[8,128]{1,0:T(8,128)S(1)}, u32[]{:S(2)}, u32[]{:S(2)}) collective-permute-start(f32[8,128]{1,0:T(8,128)S(1)} %collective-permute-done.6), channel_id=1, source_target_pairs={{0,2},{2,4},{4,6},{6,8},{8,10},{10,12},{12,14},{14,16},{16,18},{18... | collective-permute-start | bytes 12296 | tf_op jit(solution)/shard_map/ppermute | solution.py:20
  169.6 7.2 %collective-permute-start.9 = (f32[8,128]{1,0:T(8,128)S(1)}, f32[8,128]{1,0:T(8,128)S(1)}, u32[]{:S(2)}, u32[]{:S(2)}) collective-permute-start(f32[8,128]{1,0:T(8,128)S(1)} %collective-permute-done.7), channel_id=1, source_target_pairs={{0,30},{2,0},{4,2},{6,4},{8,6},{10,8},{12,10},{14,12},{16,14},{18,... | collective-permute-start | bytes 12296 | tf_op jit(solution)/shard_map/ppermute | solution.py:23
  176.8 7.2 %collective-permute-start.10 = (f32[8,128]{1,0:T(8,128)S(1)}, f32[8,128]{1,0:T(8,128)S(1)}, u32[]{:S(2)}, u32[]{:S(2)}) collective-permute-start(f32[8,128]{1,0:T(8,128)S(1)} %collective-permute-done.8), channel_id=1, source_target_pairs={{0,2},{2,4},{4,6},{6,8},{8,10},{10,12},{12,14},{14,16},{16,18},{18... | collective-permute-start | bytes 12296 | tf_op jit(solution)/shard_map/ppermute | solution.py:20
  176.8 7.2 %collective-permute-start.11 = (f32[8,128]{1,0:T(8,128)S(1)}, f32[8,128]{1,0:T(8,128)S(1)}, u32[]{:S(2)}, u32[]{:S(2)}) collective-permute-start(f32[8,128]{1,0:T(8,128)S(1)} %collective-permute-done.9), channel_id=1, source_target_pairs={{0,30},{2,0},{4,2},{6,4},{8,6},{10,8},{12,10},{14,12},{16,14},{18,... | collective-permute-start | bytes 12296 | tf_op jit(solution)/shard_map/ppermute | solution.py:23
  184.0 7.2 %collective-permute-start.12 = (f32[8,128]{1,0:T(8,128)S(1)}, f32[8,128]{1,0:T(8,128)S(1)}, u32[]{:S(2)}, u32[]{:S(2)}) collective-permute-start(f32[8,128]{1,0:T(8,128)S(1)} %collective-permute-done.10), channel_id=1, source_target_pairs={{0,2},{2,4},{4,6},{6,8},{8,10},{10,12},{12,14},{14,16},{16,18},{18... | collective-permute-start | bytes 12296 | tf_op jit(solution)/shard_map/ppermute | solution.py:20
  184.0 7.2 %collective-permute-start.13 = (f32[8,128]{1,0:T(8,128)S(1)}, f32[8,128]{1,0:T(8,128)S(1)}, u32[]{:S(2)}, u32[]{:S(2)}) collective-permute-start(f32[8,128]{1,0:T(8,128)S(1)} %collective-permute-done.11), channel_id=1, source_target_pairs={{0,30},{2,0},{4,2},{6,4},{8,6},{10,8},{12,10},{14,12},{16,14},{18,... | collective-permute-start | bytes 12296 | tf_op jit(solution)/shard_map/ppermute | solution.py:23
  191.2 7.2 %collective-permute-start.14 = (f32[8,128]{1,0:T(8,128)S(1)}, f32[8,128]{1,0:T(8,128)S(1)}, u32[]{:S(2)}, u32[]{:S(2)}) collective-permute-start(f32[8,128]{1,0:T(8,128)S(1)} %collective-permute-done.12), channel_id=1, source_target_pairs={{0,2},{2,4},{4,6},{6,8},{8,10},{10,12},{12,14},{14,16},{16,18},{18... | collective-permute-start | bytes 12296 | tf_op jit(solution)/shard_map/ppermute | solution.py:20
  218.3 5.5 collective-permute-start.15
  219.2 180.1 %all-reduce.6.cloned.1.call-start = ((), (), s32[]{:S(2)}) async-start(), calls=%async_computation.9 | async-start | bytes 131072 | tf_op jit(solution)/shard_map/psum | solution.py:83
  219.4 7.4 %collective-permute-start.16 = (bf16[2,256,128]{1,2,0:T(8,128)(2,1)}, bf16[2,256,128]{1,2,0:T(8,128)(2,1)}, u32[]{:S(2)}, u32[]{:S(2)}) collective-permute-start(bf16[2,256,128]{1,2,0:T(8,128)(2,1)} %get-tuple-element.30), channel_id=1, source_target_pairs={{0,4},{2,6},{4,0},{6,2},{8,12},{10,14},{12,8},{14,10},{16,20},{18,... | collective-permute-start | bytes 393224 | tf_op jit(solution)/shard_map/ppermute | solution.py:31
  219.5 11.1 %collective-permute-start.17 = (bf16[2,256,128]{1,2,0:T(8,128)(2,1)}, bf16[2,256,128]{1,2,0:T(8,128)(2,1)}, u32[]{:S(2)}, u32[]{:S(2)}) collective-permute-start(bf16[2,256,128]{1,2,0:T(8,128)(2,1)} %get-tuple-element.29), channel_id=1, source_target_pairs={{0,8},{2,10},{4,12},{6,14},{8,0},{10,2},{12,4},{14,6},{16,24},{18,... | collective-permute-start | bytes 393224 | tf_op jit(solution)/shard_map/ppermute | solution.py:31
  219.6 14.8 %collective-permute-start.18 = (bf16[2,256,128]{1,2,0:T(8,128)(2,1)}, bf16[2,256,128]{1,2,0:T(8,128)(2,1)S(1)}, u32[]{:S(2)}, u32[]{:S(2)}) collective-permute-start(bf16[2,256,128]{1,2,0:T(8,128)(2,1)} %get-tuple-element.28), channel_id=1, source_target_pairs={{0,16},{2,18},{4,20},{6,22},{8,24},{10,26},{12,28},{14,30},{16,0},... | collective-permute-start | bytes 393224 | tf_op jit(solution)/shard_map/ppermute | solution.py:31
  301.3 157.3 %all-gather.9.cloned.1.call-start = ((), (), s32[]{:S(2)}) async-start(), calls=%async_computation.8 | async-start | bytes 1572864 | tf_op jit(solution)/shard_map/all_gather | solution.py:38
  400.3 7.2 %collective-permute-start.19 = (f32[8,128]{1,0:T(8,128)S(1)}, f32[8,128]{1,0:T(8,128)S(1)}, u32[]{:S(2)}, u32[]{:S(2)}) collective-permute-start(f32[8,128]{1,0:T(8,128)S(1)} %get-tuple-element.38), channel_id=1, source_target_pairs={{0,2},{2,4},{4,6},{6,8},{8,10},{10,12},{12,14},{14,16},{16,18},{18... | collective-permute-start | bytes 12296 | tf_op jit(solution)/shard_map/ppermute | solution.py:20
  401.8 141.9 %all-gather.11.cloned.1.call-start = ((), (), s32[]{:S(2)}) async-start(), calls=%async_computation.10 | async-start | bytes 1572864 | tf_op jit(solution)/shard_map/all_gather | solution.py:38
  401.9 5.7 collective-permute-start.20
  407.5 7.2 %collective-permute-start.21 = (f32[8,128]{1,0:T(8,128)S(1)}, f32[8,128]{1,0:T(8,128)S(1)}, u32[]{:S(2)}, u32[]{:S(2)}) collective-permute-start(f32[8,128]{1,0:T(8,128)S(1)} %collective-permute-done.19), channel_id=1, source_target_pairs={{0,2},{2,4},{4,6},{6,8},{8,10},{10,12},{12,14},{14,16},{16,18},{18... | collective-permute-start | bytes 12296 | tf_op jit(solution)/shard_map/ppermute | solution.py:20
  407.5 7.2 %collective-permute-start.22 = (f32[8,128]{1,0:T(8,128)S(1)}, f32[8,128]{1,0:T(8,128)S(1)}, u32[]{:S(2)}, u32[]{:S(2)}) collective-permute-start(f32[8,128]{1,0:T(8,128)S(1)} %collective-permute-done.20), channel_id=1, source_target_pairs={{0,30},{2,0},{4,2},{6,4},{8,6},{10,8},{12,10},{14,12},{16,14},{18,... | collective-permute-start | bytes 12296 | tf_op jit(solution)/shard_map/ppermute | solution.py:23
  414.7 7.2 %collective-permute-start.23 = (f32[8,128]{1,0:T(8,128)S(1)}, f32[8,128]{1,0:T(8,128)S(1)}, u32[]{:S(2)}, u32[]{:S(2)}) collective-permute-start(f32[8,128]{1,0:T(8,128)S(1)} %collective-permute-done.21), channel_id=1, source_target_pairs={{0,2},{2,4},{4,6},{6,8},{8,10},{10,12},{12,14},{14,16},{16,18},{18... | collective-permute-start | bytes 12296 | tf_op jit(solution)/shard_map/ppermute | solution.py:20
  414.7 7.2 %collective-permute-start.24 = (f32[8,128]{1,0:T(8,128)S(1)}, f32[8,128]{1,0:T(8,128)S(1)}, u32[]{:S(2)}, u32[]{:S(2)}) collective-permute-start(f32[8,128]{1,0:T(8,128)S(1)} %collective-permute-done.22), channel_id=1, source_target_pairs={{0,30},{2,0},{4,2},{6,4},{8,6},{10,8},{12,10},{14,12},{16,14},{18,... | collective-permute-start | bytes 12296 | tf_op jit(solution)/shard_map/ppermute | solution.py:23
  421.9 7.2 %collective-permute-start.25 = (f32[8,128]{1,0:T(8,128)S(1)}, f32[8,128]{1,0:T(8,128)S(1)}, u32[]{:S(2)}, u32[]{:S(2)}) collective-permute-start(f32[8,128]{1,0:T(8,128)S(1)} %collective-permute-done.23), channel_id=1, source_target_pairs={{0,2},{2,4},{4,6},{6,8},{8,10},{10,12},{12,14},{14,16},{16,18},{18... | collective-permute-start | bytes 12296 | tf_op jit(solution)/shard_map/ppermute | solution.py:20
  421.9 7.2 %collective-permute-start.26 = (f32[8,128]{1,0:T(8,128)S(1)}, f32[8,128]{1,0:T(8,128)S(1)}, u32[]{:S(2)}, u32[]{:S(2)}) collective-permute-start(f32[8,128]{1,0:T(8,128)S(1)} %collective-permute-done.24), channel_id=1, source_target_pairs={{0,30},{2,0},{4,2},{6,4},{8,6},{10,8},{12,10},{14,12},{16,14},{18,... | collective-permute-start | bytes 12296 | tf_op jit(solution)/shard_map/ppermute | solution.py:23
  429.1 7.2 %collective-permute-start.27 = (f32[8,128]{1,0:T(8,128)S(1)}, f32[8,128]{1,0:T(8,128)S(1)}, u32[]{:S(2)}, u32[]{:S(2)}) collective-permute-start(f32[8,128]{1,0:T(8,128)S(1)} %collective-permute-done.25), channel_id=1, source_target_pairs={{0,2},{2,4},{4,6},{6,8},{8,10},{10,12},{12,14},{14,16},{16,18},{18... | collective-permute-start | bytes 12296 | tf_op jit(solution)/shard_map/ppermute | solution.py:20
  429.1 7.2 %collective-permute-start.28 = (f32[8,128]{1,0:T(8,128)S(1)}, f32[8,128]{1,0:T(8,128)S(1)}, u32[]{:S(2)}, u32[]{:S(2)}) collective-permute-start(f32[8,128]{1,0:T(8,128)S(1)} %collective-permute-done.26), channel_id=1, source_target_pairs={{0,30},{2,0},{4,2},{6,4},{8,6},{10,8},{12,10},{14,12},{16,14},{18,... | collective-permute-start | bytes 12296 | tf_op jit(solution)/shard_map/ppermute | solution.py:23
  436.3 7.2 %collective-permute-start.29 = (f32[8,128]{1,0:T(8,128)S(1)}, f32[8,128]{1,0:T(8,128)S(1)}, u32[]{:S(2)}, u32[]{:S(2)}) collective-permute-start(f32[8,128]{1,0:T(8,128)S(1)} %collective-permute-done.27), channel_id=1, source_target_pairs={{0,2},{2,4},{4,6},{6,8},{8,10},{10,12},{12,14},{14,16},{16,18},{18... | collective-permute-start | bytes 12296 | tf_op jit(solution)/shard_map/ppermute | solution.py:20
  436.4 7.2 %collective-permute-start.30 = (f32[8,128]{1,0:T(8,128)S(1)}, f32[8,128]{1,0:T(8,128)S(1)}, u32[]{:S(2)}, u32[]{:S(2)}) collective-permute-start(f32[8,128]{1,0:T(8,128)S(1)} %collective-permute-done.28), channel_id=1, source_target_pairs={{0,30},{2,0},{4,2},{6,4},{8,6},{10,8},{12,10},{14,12},{16,14},{18,... | collective-permute-start | bytes 12296 | tf_op jit(solution)/shard_map/ppermute | solution.py:23
  443.6 7.2 %collective-permute-start.31 = (f32[8,128]{1,0:T(8,128)S(1)}, f32[8,128]{1,0:T(8,128)S(1)}, u32[]{:S(2)}, u32[]{:S(2)}) collective-permute-start(f32[8,128]{1,0:T(8,128)S(1)} %collective-permute-done.29), channel_id=1, source_target_pairs={{0,2},{2,4},{4,6},{6,8},{8,10},{10,12},{12,14},{14,16},{16,18},{18... | collective-permute-start | bytes 12296 | tf_op jit(solution)/shard_map/ppermute | solution.py:20
  443.6 7.2 %collective-permute-start.32 = (f32[8,128]{1,0:T(8,128)S(1)}, f32[8,128]{1,0:T(8,128)S(1)}, u32[]{:S(2)}, u32[]{:S(2)}) collective-permute-start(f32[8,128]{1,0:T(8,128)S(1)} %collective-permute-done.30), channel_id=1, source_target_pairs={{0,30},{2,0},{4,2},{6,4},{8,6},{10,8},{12,10},{14,12},{16,14},{18,... | collective-permute-start | bytes 12296 | tf_op jit(solution)/shard_map/ppermute | solution.py:23
  450.8 7.2 %collective-permute-start.33 = (f32[8,128]{1,0:T(8,128)S(1)}, f32[8,128]{1,0:T(8,128)S(1)}, u32[]{:S(2)}, u32[]{:S(2)}) collective-permute-start(f32[8,128]{1,0:T(8,128)S(1)} %collective-permute-done.31), channel_id=1, source_target_pairs={{0,2},{2,4},{4,6},{6,8},{8,10},{10,12},{12,14},{14,16},{16,18},{18... | collective-permute-start | bytes 12296 | tf_op jit(solution)/shard_map/ppermute | solution.py:20
  523.0 5.1 collective-permute-start.34
  525.2 5.8 collective-permute-start.35
  525.2 9.5 %collective-permute-start.36 = (bf16[2,256,128]{1,2,0:T(8,128)(2,1)}, bf16[2,256,128]{1,2,0:T(8,128)(2,1)}, u32[]{:S(2)}, u32[]{:S(2)}) collective-permute-start(bf16[2,256,128]{1,2,0:T(8,128)(2,1)} %get-tuple-element.21), channel_id=1, source_target_pairs={{0,8},{2,10},{4,12},{6,14},{8,0},{10,2},{12,4},{14,6},{16,24},{18,... | collective-permute-start | bytes 393224 | tf_op jit(solution)/shard_map/ppermute | solution.py:31
  525.3 13.2 %collective-permute-start.37 = (bf16[2,256,128]{1,2,0:T(8,128)(2,1)}, bf16[2,256,128]{1,2,0:T(8,128)(2,1)S(1)}, u32[]{:S(2)}, u32[]{:S(2)}) collective-permute-start(bf16[2,256,128]{1,2,0:T(8,128)(2,1)} %get-tuple-element.20), channel_id=1, source_target_pairs={{0,16},{2,18},{4,20},{6,22},{8,24},{10,26},{12,28},{14,30},{16,0},... | collective-permute-start | bytes 393224 | tf_op jit(solution)/shard_map/ppermute | solution.py:31
  (13 other events, 309.6 us)
Sparse Core Ops, SparseCore 0:
  39.4 100.3 all-reduce.3
  301.5 97.8 all-reduce.5
Sparse Core Ops, SparseCore 1:
  146.6 5.2 all-gather.4
  219.3 6.7 all-gather.6
  401.9 8.8 all-gather.8
  525.2 5.1 all-gather.10
